TPU v7x, 32 devices: a whole 2x2x4 slice. The times are simulated.
32 devices in a mesh: grp: 2 (over y), sx: 4 (over x, core), sy: 4 (over z).
Axes of the slice: x: 2, y: 2, z: 4, core: 2. Of those that a mesh axis runs over, the one named last changes fastest.
Arguments:
- rhs_field: float32 [64, 64, 512], P(('grp', 'sx'), None, 'sy'), parts along dimension 0, may hold values from -6 to 6
- conduct: float32 [64, 64, 512], P(('grp', 'sx'), None, 'sy'), parts along dimension 0, may hold values from 0.05 to 5
- intersections: int32 [8, 2], P('grp'), parts along dimension 0, may hold values from 1 to 4, as said below
- poly_coef: float32 [4], replicated
Outputs:
- solution_field: float32 [64, 64, 512], P(('grp', 'sx'), None, 'sy'), parts along dimension 0
- residual: float32 [64, 64, 512], P(('grp', 'sx'), None, 'sy'), parts along dimension 0
There are 2 independent parts, one for each index of `grp`. A program takes and returns all parts, laid end to end along the dimension named above; an argument that names none is the same for every part. Nothing has to cross between parts.
Inputs may be any that keep to these rules, and one draw needn't show every extreme that they name: `intersections`: 4 is reached in every draw.
All inputs are finite; a program needn't handle non-finite values.
Results may differ from a plain program's by a relative error of at most 0.0003.
Values sent between devices are 32-bit elements; how exact they have to be, the bound alone decides.
A program may use at most 128 MiB of HBM per device.

v0:
```python
import jax
import jax.numpy as jnp
from jax import lax
from jax.sharding import PartitionSpec as P

OV = 4
DEG = 3
M = 4


def extended(shard, sides, width):
    for axis, dim in sides:
        size, length = (lax.axis_size(axis), shard.shape[dim])
        up = [(i, (i + 1) % size) for i in range(size - 1)]
        down = [(j, i) for i, j in up]
        last = lax.slice_in_dim(shard, length - width, length, axis=dim)
        initial = lax.slice_in_dim(shard, 0, width, axis=dim)
        before = lax.ppermute(last, axis, up)
        after = lax.ppermute(initial, axis, down)
        shard = jnp.concatenate([before, shard, after], axis=dim)
    return shard


def five_point_operator(padded_vector, padded_krylov):
    center_krylov = padded_krylov[1:-1, :, 1:-1]
    center_vector = padded_vector[1:-1, :, 1:-1]
    grand_total = (
        0.5
        * (center_krylov + padded_krylov[2:, :, 1:-1])
        * (center_vector - padded_vector[2:, :, 1:-1])
    )
    grand_total = grand_total + 0.5 * (center_krylov + padded_krylov[:-2, :, 1:-1]) * (
        center_vector - padded_vector[:-2, :, 1:-1]
    )
    grand_total = grand_total + 0.5 * (center_krylov + padded_krylov[1:-1, :, 2:]) * (
        center_vector - padded_vector[1:-1, :, 2:]
    )
    grand_total = grand_total + 0.5 * (center_krylov + padded_krylov[1:-1, :, :-2]) * (
        center_vector - padded_vector[1:-1, :, :-2]
    )
    kvert = jnp.pad(center_krylov, ((0, 0), (1, 1), (0, 0)))
    vvert = jnp.pad(center_vector, ((0, 0), (1, 1), (0, 0)))
    grand_total = grand_total + 0.5 * (center_krylov + kvert[:, 2:]) * (
        center_vector - vvert[:, 2:]
    )
    grand_total = grand_total + 0.5 * (center_krylov + kvert[:, :-2]) * (
        center_vector - vvert[:, :-2]
    )
    return grand_total


def diagonal(padded_krylov):
    center_krylov = padded_krylov[1:-1, :, 1:-1]
    kvert = jnp.pad(center_krylov, ((0, 0), (1, 1), (0, 0)))
    grand_total = 0.5 * (center_krylov + padded_krylov[2:, :, 1:-1]) + 0.5 * (
        center_krylov + padded_krylov[:-2, :, 1:-1]
    )
    grand_total = (
        grand_total
        + 0.5 * (center_krylov + padded_krylov[1:-1, :, 2:])
        + 0.5 * (center_krylov + padded_krylov[1:-1, :, :-2])
    )
    grand_total = (
        grand_total + 0.5 * (center_krylov + kvert[:, 2:]) + 0.5 * (center_krylov + kvert[:, :-2])
    )
    return jnp.where(center_krylov > 0, grand_total, 1.0)


def least_squares(hmat, beta):
    rows = hmat
    target = jnp.zeros((M + 1,), jnp.float32).at[0].set(beta)
    for step in range(M):
        first = rows[step, step]
        second = rows[step + 1, step]
        radius = jnp.sqrt(first * first + second * second)
        cosine = first / radius
        sine_val = second / radius
        upper = cosine * rows[step] + sine_val * rows[step + 1]
        lower = -sine_val * rows[step] + cosine * rows[step + 1]
        rows = rows.at[step].set(upper).at[step + 1].set(lower)
        tgt_up = cosine * target[step] + sine_val * target[step + 1]
        tgt_low = -sine_val * target[step] + cosine * target[step + 1]
        target = target.at[step].set(tgt_up).at[step + 1].set(tgt_low)
    coeffs = [None] * M
    for step in reversed(range(M)):
        running = target[step]
        for later in range(step + 1, M):
            running = running - rows[step, later] * coeffs[later]
        coeffs[step] = running / rows[step, step]
    return coeffs


def local(rhs_field, conduct, intersections, poly_coef):
    width_x = rhs_field.shape[0]
    vertical_width = rhs_field.shape[2]
    extent = width_x + 2 * OV
    kfull = extended(conduct, (("sx", 0), ("sy", 2)), OV + 1)
    kglobal = kfull[OV : OV + width_x + 2, :, OV : OV + vertical_width + 2]
    kdeep = kfull[:, :, OV - DEG : OV + vertical_width + DEG + 2]
    ddeep = diagonal(kdeep)
    subdomain = lax.axis_index("sx")
    count_x = lax.axis_size("sx")
    strip_index = lax.axis_index("sy")
    count_y = lax.axis_size("sy")
    own_row = lax.dynamic_slice_in_dim(intersections, subdomain, 1, 0)
    left = own_row[0, 0]
    right = own_row[0, 1]
    plane = jnp.arange(extent, dtype=jnp.int32)
    gpos = subdomain * width_x + plane - OV
    keep = (
        (plane >= OV - left)
        & (plane < OV + width_x + right)
        & (gpos >= 0)
        & (gpos < width_x * count_x)
    )
    keep = keep[:, None, None]
    column = jnp.arange(vertical_width + 2 * DEG, dtype=jnp.int32)
    ycol = strip_index * vertical_width + column - DEG
    inside_y = (ycol >= 0) & (ycol < vertical_width * count_y)
    inside_y = inside_y[None, None, :]

    def operator(field):
        padded = extended(field, (("sx", 0), ("sy", 2)), 1)
        return five_point_operator(padded, kglobal)

    def precondition(resid):
        slab = extended(resid, (("sx", 0),), OV)
        wide = extended(slab, (("sy", 2),), DEG)
        level = jnp.where(keep & inside_y, wide / ddeep, 0.0)
        result = poly_coef[0] * level[OV : OV + width_x, :, DEG : DEG + vertical_width]
        for power in range(1, DEG + 1):
            span = vertical_width + 2 * (DEG - power)
            padded = jnp.pad(level, ((1, 1), (0, 0), (0, 0)))
            mask_now = keep & inside_y[:, :, power : power + span]
            level = jnp.where(
                mask_now,
                five_point_operator(padded, kdeep[:, :, power : power + span + 2])
                / ddeep[:, :, power : power + span],
                0.0,
            )
            margin = DEG - power
            result = (
                result
                + poly_coef[power] * level[OV : OV + width_x, :, margin : margin + vertical_width]
            )
        return result

    beta = jnp.sqrt(lax.psum(jnp.sum(rhs_field * rhs_field), ("sx", "sy")))
    basis = [rhs_field / beta]
    kept_vectors = []
    columns = []
    for step in range(M):
        precond_vec = precondition(basis[step])
        kept_vectors.append(precond_vec)
        image = operator(precond_vec)
        local_dots = jnp.stack([jnp.sum(image * vec) for vec in basis])
        proj = lax.psum(local_dots, ("sx", "sy"))
        for which in range(step + 1):
            image = image - proj[which] * basis[which]
        new_len = jnp.sqrt(lax.psum(jnp.sum(image * image), ("sx", "sy")))
        basis.append(image / new_len)
        entries = (
            [proj[which] for which in range(step + 1)]
            + [new_len]
            + [jnp.zeros((), jnp.float32)] * (M - step - 1)
        )
        columns.append(jnp.stack(entries))
    hmat = jnp.stack(columns, axis=1)
    coeffs = least_squares(hmat, beta)
    combined = coeffs[0] * basis[0]
    for step in range(1, M):
        combined = combined + coeffs[step] * basis[step]
    solution_field = precondition(combined)
    residual = rhs_field - operator(solution_field)
    return (solution_field, residual)


def solution(mesh):
    in_specs = (P(("grp", "sx"), None, "sy"), P(("grp", "sx"), None, "sy"), P("grp", None), P())
    out_specs = (P(("grp", "sx"), None, "sy"), P(("grp", "sx"), None, "sy"))
    return jax.shard_map(local, mesh=mesh, in_specs=in_specs, out_specs=out_specs, check_vma=False)
```

profile of v0, /device:TPU:0, one launch (start us, length us, event | category | flops | bytes accessed | tf_op | source)
XLA Modules:
  0.0 671.9 jit_solution(8221359077134430371)
XLA Ops:
  7.0 36.6 %psum.63 = f32[]{:T(128)} all-reduce(f32[]{:T(128)} %multiply_reduce_fusion.14), channel_id=1, replica_groups=mesh['grp'=2,'sx'=4,'sy'=4] {'sx','sy'}, use_global_device_ids=true, to_apply=%region_1.2 | all-reduce | flops 1 | bytes 8 | tf_op jit(solution)/shard_map/psum | solution.py:148
  46.6 3.0 collective-permute-start.1
  60.1 6.0 collective-permute-start.3
  68.5 7.7 %collective-permute-done.4 = f32[16,64,3]{2,1,0:T(8,128)} collective-permute-done((f32[16,64,3]{2,1,0:T(8,128)}, f32[16,64,3]{2,1,0:T(8,128)}, u32[]{:S(2)}, u32[]{:S(2)}) %collective-permute-start.4) | collective-permute-done | bytes 12320 | tf_op jit(solution)/shard_map/ppermute | solution.py:19
  81.1 4.3 fusion.203
  86.5 4.4 fusion.202
  98.3 3.0 collective-permute-start.9
  102.4 4.4 collective-permute-start.11
  108.1 6.3 collective-permute-done.11
  114.4 4.6 collective-permute-done.10
  121.4 32.4 %psum.64 = f32[1]{0:T(128)} all-reduce(f32[1]{0:T(128)} %bitcast.7), channel_id=1, replica_groups=mesh['grp'=2,'sx'=4,'sy'=4] {'sx','sy'}, use_global_device_ids=true, to_apply=%region_3.4 | all-reduce | flops 1 | bytes 8 | tf_op jit(solution)/shard_map/psum | solution.py:157
  156.0 30.6 %psum.65 = f32[]{:T(128)} all-reduce(f32[]{:T(128)} %multiply_reduce_fusion.12), channel_id=1, replica_groups=mesh['grp'=2,'sx'=4,'sy'=4] {'sx','sy'}, use_global_device_ids=true, to_apply=%region_5.6 | all-reduce | flops 1 | bytes 8 | tf_op jit(solution)/shard_map/psum | solution.py:160
  190.2 3.0 collective-permute-start.12
  195.8 4.7 collective-permute-start.14
  200.5 10.3 %collective-permute-done.15 = f32[16,64,3]{2,1,0:T(8,128)S(1)} collective-permute-done((f32[16,64,3]{2,1,0:T(8,128)S(1)}, f32[16,64,3]{2,1,0:T(8,128)S(1)}, u32[]{:S(2)}, u32[]{:S(2)}) %collective-permute-start.15) | collective-permute-done | bytes 12320 | tf_op jit(solution)/shard_map/ppermute | solution.py:19
  226.0 3.0 collective-permute-start.17
  230.1 4.4 collective-permute-start.19
  235.8 6.3 collective-permute-done.19
  242.0 4.7 collective-permute-done.18
  249.8 31.9 %psum.66 = f32[2]{0:T(128)S(1)} all-reduce(f32[2]{0:T(128)S(1)} %pad_maximum_fusion.58), channel_id=1, replica_groups=mesh['grp'=2,'sx'=4,'sy'=4] {'sx','sy'}, use_global_device_ids=true, to_apply=%region_8.9 | all-reduce | flops 2 | bytes 16 | tf_op jit(solution)/shard_map/psum | solution.py:157
  285.1 30.4 %psum.67 = f32[]{:T(128)} all-reduce(f32[]{:T(128)} %get-tuple-element.221), channel_id=1, replica_groups=mesh['grp'=2,'sx'=4,'sy'=4] {'sx','sy'}, use_global_device_ids=true, to_apply=%region_10.11 | all-reduce | flops 1 | bytes 8 | tf_op jit(solution)/shard_map/psum | solution.py:160
  317.5 3.0 collective-permute-start.20
  323.1 4.9 collective-permute-start.22
  328.0 10.0 %collective-permute-done.23 = f32[16,64,3]{2,1,0:T(8,128)S(1)} collective-permute-done((f32[16,64,3]{2,1,0:T(8,128)S(1)}, f32[16,64,3]{2,1,0:T(8,128)S(1)}, u32[]{:S(2)}, u32[]{:S(2)}) %collective-permute-start.23) | collective-permute-done | bytes 12320 | tf_op jit(solution)/shard_map/ppermute | solution.py:19
  353.3 3.0 collective-permute-start.25
  357.4 4.4 collective-permute-start.27
  363.1 6.3 collective-permute-done.27
  369.4 4.6 collective-permute-done.26
  377.7 31.9 %psum.68 = f32[3]{0:T(128)S(1)} all-reduce(f32[3]{0:T(128)S(1)} %pad_maximum_fusion.59), channel_id=1, replica_groups=mesh['grp'=2,'sx'=4,'sy'=4] {'sx','sy'}, use_global_device_ids=true, to_apply=%region_14.15 | all-reduce | flops 3 | bytes 24 | tf_op jit(solution)/shard_map/psum | solution.py:157
  410.3 4.4 multiply_reduce_fusion.5
  414.6 30.4 %psum.69 = f32[]{:T(128)} all-reduce(f32[]{:T(128)} %get-tuple-element.218), channel_id=1, replica_groups=mesh['grp'=2,'sx'=4,'sy'=4] {'sx','sy'}, use_global_device_ids=true, to_apply=%region_16.17 | all-reduce | flops 1 | bytes 8 | tf_op jit(solution)/shard_map/psum | solution.py:160
  448.0 3.0 collective-permute-start.28
  453.6 4.7 collective-permute-start.30
  458.3 10.2 %collective-permute-done.31 = f32[16,64,3]{2,1,0:T(8,128)S(1)} collective-permute-done((f32[16,64,3]{2,1,0:T(8,128)S(1)}, f32[16,64,3]{2,1,0:T(8,128)S(1)}, u32[]{:S(2)}, u32[]{:S(2)}) %collective-permute-start.31) | collective-permute-done | bytes 12320 | tf_op jit(solution)/shard_map/ppermute | solution.py:19
  484.3 3.3 collective-permute-start.33
  493.3 5.1 collective-permute-start.35
  500.4 5.4 collective-permute-done.35
  505.8 5.3 collective-permute-done.34
  511.1 4.2 multiply_reduce_fusion.4
  518.6 31.1 %psum.70 = f32[4]{0:T(128)S(1)} all-reduce(f32[4]{0:T(128)S(1)} %pad_maximum_fusion.60), channel_id=1, replica_groups=mesh['grp'=2,'sx'=4,'sy'=4] {'sx','sy'}, use_global_device_ids=true, to_apply=%region_21.22 | all-reduce | flops 4 | bytes 32 | tf_op jit(solution)/shard_map/psum | solution.py:157
  550.3 4.2 multiply_reduce_fusion
  554.6 31.1 %psum.71 = f32[]{:T(128)} all-reduce(f32[]{:T(128)} %multiply_reduce_fusion), channel_id=1, replica_groups=mesh['grp'=2,'sx'=4,'sy'=4] {'sx','sy'}, use_global_device_ids=true, to_apply=%region_23.24 | all-reduce | flops 1 | bytes 8 | tf_op jit(solution)/shard_map/psum | solution.py:160
  613.7 3.0 collective-permute-start.36
  619.2 4.6 collective-permute-start.38
  623.8 10.8 %collective-permute-done.39 = f32[16,64,3]{2,1,0:T(8,128)S(1)} collective-permute-done((f32[16,64,3]{2,1,0:T(8,128)S(1)}, f32[16,64,3]{2,1,0:T(8,128)S(1)}, u32[]{:S(2)}, u32[]{:S(2)}) %collective-permute-start.39) | collective-permute-done | bytes 12320 | tf_op jit(solution)/shard_map/ppermute | solution.py:19
  653.5 4.4 collective-permute-start.43
  659.2 6.5 collective-permute-done.43
  665.7 4.7 collective-permute-done.42
  (417 shorter events, 155.8 us)
Async XLA Ops:
  0.6 49.3 %copy-start = (s32[4,2]{0,1:T(2,128)S(1)}, s32[4,2]{0,1:T(2,128)}, u32[]{:S(2)}) copy-start(s32[4,2]{0,1:T(2,128)} %param.40) | copy-start | bytes 100
  0.6 51.5 %copy-start.108 = (f32[4]{0:T(128)S(1)}, f32[4]{0:T(128)}, u32[]{:S(2)}) copy-start(f32[4]{0:T(128)} %param.41) | copy-start | bytes 52
  1.7 51.8 %collective-permute-start.5 = (f32[5,64,128]{2,1,0:T(8,128)S(1)}, f32[5,64,128]{2,1,0:T(8,128)S(1)}, u32[]{:S(2)}, u32[]{:S(2)}) collective-permute-start(f32[5,64,128]{2,1,0:T(8,128)S(1)} %get-tuple-element.335), channel_id=1, source_target_pairs={{0,4},{4,8},{8,12},{1,5},{5,9},{9,13},{2,6},{6,10},{10,14},{3,7},{... | collective-permute-start | bytes 491528 | tf_op jit(solution)/shard_map/ppermute | solution.py:18
  5.7 47.9 %collective-permute-start = (f32[5,64,128]{2,1,0:T(8,128)S(1)}, f32[5,64,128]{2,1,0:T(8,128)S(1)}, u32[]{:S(2)}, u32[]{:S(2)}) collective-permute-start(f32[5,64,128]{2,1,0:T(8,128)S(1)} %get-tuple-element.334), channel_id=1, source_target_pairs={{4,0},{8,4},{12,8},{5,1},{9,5},{13,9},{6,2},{10,6},{14,10},{7,3},{... | collective-permute-start | bytes 491528 | tf_op jit(solution)/shard_map/ppermute | solution.py:19
  45.3 7.5 %collective-permute-start.2 = (f32[4,64,128]{2,1,0:T(8,128)S(1)}, f32[4,64,128]{2,1,0:T(8,128)S(1)}, u32[]{:S(2)}, u32[]{:S(2)}) collective-permute-start(f32[4,64,128]{2,1,0:T(8,128)S(1)} %get-tuple-element.337), channel_id=1, source_target_pairs={{4,0},{8,4},{12,8},{5,1},{9,5},{13,9},{6,2},{10,6},{14,10},{7,3},{... | collective-permute-start | bytes 393224 | tf_op jit(solution)/shard_map/ppermute | solution.py:19
  46.6 6.3 collective-permute-start.1
  54.8 11.3 %collective-permute-start.6 = (f32[18,64,5]{1,0,2:T(8,128)S(1)}, f32[18,64,5]{1,0,2:T(8,128)S(1)}, u32[]{:S(2)}, u32[]{:S(2)}) collective-permute-start(f32[18,64,5]{1,0,2:T(8,128)S(1)} %copy.28), channel_id=1, source_target_pairs={{0,1},{1,2},{2,3},{4,5},{5,6},{6,7},{8,9},{9,10},{10,11},{12,13},{... | collective-permute-start | bytes 69128 | tf_op jit(solution)/shard_map/ppermute | solution.py:18
  56.4 10.0 %collective-permute-start.7 = (f32[18,64,5]{1,0,2:T(8,128)S(1)}, f32[18,64,5]{1,0,2:T(8,128)S(1)}, u32[]{:S(2)}, u32[]{:S(2)}) collective-permute-start(f32[18,64,5]{1,0,2:T(8,128)S(1)} %copy.29), channel_id=1, source_target_pairs={{1,0},{2,1},{3,2},{5,4},{6,5},{7,6},{9,8},{10,9},{11,10},{13,12},{... | collective-permute-start | bytes 69128 | tf_op jit(solution)/shard_map/ppermute | solution.py:19
  58.8 17.3 %collective-permute-start.4 = (f32[16,64,3]{2,1,0:T(8,128)}, f32[16,64,3]{2,1,0:T(8,128)}, u32[]{:S(2)}, u32[]{:S(2)}) collective-permute-start(f32[16,64,3]{2,1,0:T(8,128)} %get-tuple-element.305), channel_id=1, source_target_pairs={{1,0},{2,1},{3,2},{5,4},{6,5},{7,6},{9,8},{10,9},{11,10},{13,12},{... | collective-permute-start | bytes 36872 | tf_op jit(solution)/shard_map/ppermute | solution.py:19
  60.1 17.7 %collective-permute-start.3 = (f32[16,64,3]{2,1,0:T(8,128)}, f32[16,64,3]{2,1,0:T(8,128)}, u32[]{:S(2)}, u32[]{:S(2)}) collective-permute-start(f32[16,64,3]{2,1,0:T(8,128)} %get-tuple-element.304), channel_id=1, source_target_pairs={{0,1},{1,2},{2,3},{4,5},{5,6},{6,7},{8,9},{9,10},{10,11},{12,13},{... | collective-permute-start | bytes 36872 | tf_op jit(solution)/shard_map/ppermute | solution.py:18
  96.9 4.5 collective-permute-start.8
  98.3 3.9 collective-permute-start.9
  102.4 12.0 %collective-permute-start.11 = (f32[10,64,1]{2,1,0:T(8,128)S(1)}, f32[10,64,1]{2,1,0:T(8,128)S(1)}, u32[]{:S(2)}, u32[]{:S(2)}) collective-permute-start(f32[10,64,1]{2,1,0:T(8,128)S(1)} %get-tuple-element.315), channel_id=1, source_target_pairs={{0,1},{1,2},{2,3},{4,5},{5,6},{6,7},{8,9},{9,10},{10,11},{12,13},{... | collective-permute-start | bytes 7688 | tf_op jit(solution)/shard_map/ppermute | solution.py:18
  106.8 12.2 %collective-permute-start.10 = (f32[10,64,1]{2,1,0:T(8,128)S(1)}, f32[10,64,1]{2,1,0:T(8,128)S(1)}, u32[]{:S(2)}, u32[]{:S(2)}) collective-permute-start(f32[10,64,1]{2,1,0:T(8,128)S(1)} %get-tuple-element.314), channel_id=1, source_target_pairs={{1,0},{2,1},{3,2},{5,4},{6,5},{7,6},{9,8},{10,9},{11,10},{13,12},{... | collective-permute-start | bytes 7688 | tf_op jit(solution)/shard_map/ppermute | solution.py:19
  188.9 4.3 collective-permute-start.13
  190.2 4.0 collective-permute-start.12
  194.5 16.3 %collective-permute-start.15 = (f32[16,64,3]{2,1,0:T(8,128)S(1)}, f32[16,64,3]{2,1,0:T(8,128)S(1)}, u32[]{:S(2)}, u32[]{:S(2)}) collective-permute-start(f32[16,64,3]{2,1,0:T(8,128)S(1)} %get-tuple-element.299), channel_id=1, source_target_pairs={{1,0},{2,1},{3,2},{5,4},{6,5},{7,6},{9,8},{10,9},{11,10},{13,12},{... | collective-permute-start | bytes 36872 | tf_op jit(solution)/shard_map/ppermute | solution.py:19
  195.8 16.6 %collective-permute-start.14 = (f32[16,64,3]{2,1,0:T(8,128)S(1)}, f32[16,64,3]{2,1,0:T(8,128)S(1)}, u32[]{:S(2)}, u32[]{:S(2)}) collective-permute-start(f32[16,64,3]{2,1,0:T(8,128)S(1)} %get-tuple-element.298), channel_id=1, source_target_pairs={{0,1},{1,2},{2,3},{4,5},{5,6},{6,7},{8,9},{9,10},{10,11},{12,13},{... | collective-permute-start | bytes 36872 | tf_op jit(solution)/shard_map/ppermute | solution.py:18
  224.6 4.5 collective-permute-start.16
  226.0 3.9 collective-permute-start.17
  230.1 12.0 %collective-permute-start.19 = (f32[10,64,1]{2,1,0:T(8,128)S(1)}, f32[10,64,1]{2,1,0:T(8,128)S(1)}, u32[]{:S(2)}, u32[]{:S(2)}) collective-permute-start(f32[10,64,1]{2,1,0:T(8,128)S(1)} %get-tuple-element.313), channel_id=1, source_target_pairs={{0,1},{1,2},{2,3},{4,5},{5,6},{6,7},{8,9},{9,10},{10,11},{12,13},{... | collective-permute-start | bytes 7688 | tf_op jit(solution)/shard_map/ppermute | solution.py:18
  234.5 12.3 %collective-permute-start.18 = (f32[10,64,1]{2,1,0:T(8,128)S(1)}, f32[10,64,1]{2,1,0:T(8,128)S(1)}, u32[]{:S(2)}, u32[]{:S(2)}) collective-permute-start(f32[10,64,1]{2,1,0:T(8,128)S(1)} %get-tuple-element.312), channel_id=1, source_target_pairs={{1,0},{2,1},{3,2},{5,4},{6,5},{7,6},{9,8},{10,9},{11,10},{13,12},{... | collective-permute-start | bytes 7688 | tf_op jit(solution)/shard_map/ppermute | solution.py:19
  281.6 39.9 %copy-start.112 = (f32[2]{0:T(128)}, f32[2]{0:T(128)S(1)}, u32[]{:S(2)}) copy-start(f32[2]{0:T(128)S(1)} %psum.66) | copy-start | bytes 28
  316.2 4.3 collective-permute-start.21
  317.5 4.0 collective-permute-start.20
  321.8 16.2 %collective-permute-start.23 = (f32[16,64,3]{2,1,0:T(8,128)S(1)}, f32[16,64,3]{2,1,0:T(8,128)S(1)}, u32[]{:S(2)}, u32[]{:S(2)}) collective-permute-start(f32[16,64,3]{2,1,0:T(8,128)S(1)} %get-tuple-element.295), channel_id=1, source_target_pairs={{1,0},{2,1},{3,2},{5,4},{6,5},{7,6},{9,8},{10,9},{11,10},{13,12},{... | collective-permute-start | bytes 36872 | tf_op jit(solution)/shard_map/ppermute | solution.py:19
  323.1 16.7 %collective-permute-start.22 = (f32[16,64,3]{2,1,0:T(8,128)S(1)}, f32[16,64,3]{2,1,0:T(8,128)S(1)}, u32[]{:S(2)}, u32[]{:S(2)}) collective-permute-start(f32[16,64,3]{2,1,0:T(8,128)S(1)} %get-tuple-element.294), channel_id=1, source_target_pairs={{0,1},{1,2},{2,3},{4,5},{5,6},{6,7},{8,9},{9,10},{10,11},{12,13},{... | collective-permute-start | bytes 36872 | tf_op jit(solution)/shard_map/ppermute | solution.py:18
  351.9 4.5 collective-permute-start.24
  353.3 3.9 collective-permute-start.25
  357.4 12.0 %collective-permute-start.27 = (f32[10,64,1]{2,1,0:T(8,128)S(1)}, f32[10,64,1]{2,1,0:T(8,128)S(1)}, u32[]{:S(2)}, u32[]{:S(2)}) collective-permute-start(f32[10,64,1]{2,1,0:T(8,128)S(1)} %get-tuple-element.311), channel_id=1, source_target_pairs={{0,1},{1,2},{2,3},{4,5},{5,6},{6,7},{8,9},{9,10},{10,11},{12,13},{... | collective-permute-start | bytes 7688 | tf_op jit(solution)/shard_map/ppermute | solution.py:18
  361.8 12.2 %collective-permute-start.26 = (f32[10,64,1]{2,1,0:T(8,128)S(1)}, f32[10,64,1]{2,1,0:T(8,128)S(1)}, u32[]{:S(2)}, u32[]{:S(2)}) collective-permute-start(f32[10,64,1]{2,1,0:T(8,128)S(1)} %get-tuple-element.310), channel_id=1, source_target_pairs={{1,0},{2,1},{3,2},{5,4},{6,5},{7,6},{9,8},{10,9},{11,10},{13,12},{... | collective-permute-start | bytes 7688 | tf_op jit(solution)/shard_map/ppermute | solution.py:19
  446.7 4.3 collective-permute-start.29
  448.0 4.0 collective-permute-start.28
  452.3 16.2 %collective-permute-start.31 = (f32[16,64,3]{2,1,0:T(8,128)S(1)}, f32[16,64,3]{2,1,0:T(8,128)S(1)}, u32[]{:S(2)}, u32[]{:S(2)}) collective-permute-start(f32[16,64,3]{2,1,0:T(8,128)S(1)} %get-tuple-element.291), channel_id=1, source_target_pairs={{1,0},{2,1},{3,2},{5,4},{6,5},{7,6},{9,8},{10,9},{11,10},{13,12},{... | collective-permute-start | bytes 36872 | tf_op jit(solution)/shard_map/ppermute | solution.py:19
  453.6 16.7 %collective-permute-start.30 = (f32[16,64,3]{2,1,0:T(8,128)S(1)}, f32[16,64,3]{2,1,0:T(8,128)S(1)}, u32[]{:S(2)}, u32[]{:S(2)}) collective-permute-start(f32[16,64,3]{2,1,0:T(8,128)S(1)} %get-tuple-element.290), channel_id=1, source_target_pairs={{0,1},{1,2},{2,3},{4,5},{5,6},{6,7},{8,9},{9,10},{10,11},{12,13},{... | collective-permute-start | bytes 36872 | tf_op jit(solution)/shard_map/ppermute | solution.py:18
  483.0 8.4 %collective-permute-start.32 = (f32[1,64,128]{2,1,0:T(8,128)S(1)}, f32[1,64,128]{2,1,0:T(8,128)S(1)}, u32[]{:S(2)}, u32[]{:S(2)}) collective-permute-start(f32[1,64,128]{2,1,0:T(8,128)S(1)} %get-tuple-element.321), channel_id=1, source_target_pairs={{4,0},{8,4},{12,8},{5,1},{9,5},{13,9},{6,2},{10,6},{14,10},{7,3},{... | collective-permute-start | bytes 98312 | tf_op jit(solution)/shard_map/ppermute | solution.py:19
  484.3 7.1 %collective-permute-start.33 = (f32[1,64,128]{2,1,0:T(8,128)S(1)}, f32[1,64,128]{2,1,0:T(8,128)S(1)}, u32[]{:S(2)}, u32[]{:S(2)}) collective-permute-start(f32[1,64,128]{2,1,0:T(8,128)S(1)} %get-tuple-element.320), channel_id=1, source_target_pairs={{0,4},{4,8},{8,12},{1,5},{5,9},{9,13},{2,6},{6,10},{10,14},{3,7},{... | collective-permute-start | bytes 98312 | tf_op jit(solution)/shard_map/ppermute | solution.py:18
  493.3 12.5 %collective-permute-start.35 = (f32[10,64,1]{2,1,0:T(8,128)}, f32[10,64,1]{2,1,0:T(8,128)}, u32[]{:S(2)}, u32[]{:S(2)}) collective-permute-start(f32[10,64,1]{2,1,0:T(8,128)} %get-tuple-element.309), channel_id=1, source_target_pairs={{0,1},{1,2},{2,3},{4,5},{5,6},{6,7},{8,9},{9,10},{10,11},{12,13},{... | collective-permute-start | bytes 7688 | tf_op jit(solution)/shard_map/ppermute | solution.py:18
  498.4 12.7 %collective-permute-start.34 = (f32[10,64,1]{2,1,0:T(8,128)}, f32[10,64,1]{2,1,0:T(8,128)}, u32[]{:S(2)}, u32[]{:S(2)}) collective-permute-start(f32[10,64,1]{2,1,0:T(8,128)} %get-tuple-element.308), channel_id=1, source_target_pairs={{1,0},{2,1},{3,2},{5,4},{6,5},{7,6},{9,8},{10,9},{11,10},{13,12},{... | collective-permute-start | bytes 7688 | tf_op jit(solution)/shard_map/ppermute | solution.py:19
  515.3 39.2 %copy-start.110 = (f32[3]{0:T(128)S(1)}, f32[3]{0:T(128)}, u32[]{:S(2)}) copy-start(f32[3]{0:T(128)} %copy-done.109) | copy-start | bytes 40
  612.4 4.3 collective-permute-start.37
  613.7 4.0 collective-permute-start.36
  617.9 16.7 %collective-permute-start.39 = (f32[16,64,3]{2,1,0:T(8,128)S(1)}, f32[16,64,3]{2,1,0:T(8,128)S(1)}, u32[]{:S(2)}, u32[]{:S(2)}) collective-permute-start(f32[16,64,3]{2,1,0:T(8,128)S(1)} %get-tuple-element.287), channel_id=1, source_target_pairs={{1,0},{2,1},{3,2},{5,4},{6,5},{7,6},{9,8},{10,9},{11,10},{13,12},{... | collective-permute-start | bytes 36872 | tf_op jit(solution)/shard_map/ppermute | solution.py:19
  619.2 16.6 %collective-permute-start.38 = (f32[16,64,3]{2,1,0:T(8,128)S(1)}, f32[16,64,3]{2,1,0:T(8,128)S(1)}, u32[]{:S(2)}, u32[]{:S(2)}) collective-permute-start(f32[16,64,3]{2,1,0:T(8,128)S(1)} %get-tuple-element.286), channel_id=1, source_target_pairs={{0,1},{1,2},{2,3},{4,5},{5,6},{6,7},{8,9},{9,10},{10,11},{12,13},{... | collective-permute-start | bytes 36872 | tf_op jit(solution)/shard_map/ppermute | solution.py:18
  648.0 4.5 collective-permute-start.40
  649.4 3.9 collective-permute-start.41
  653.5 12.2 %collective-permute-start.43 = (f32[10,64,1]{2,1,0:T(8,128)S(1)}, f32[10,64,1]{2,1,0:T(8,128)S(1)}, u32[]{:S(2)}, u32[]{:S(2)}) collective-permute-start(f32[10,64,1]{2,1,0:T(8,128)S(1)} %get-tuple-element.307), channel_id=1, source_target_pairs={{0,1},{1,2},{2,3},{4,5},{5,6},{6,7},{8,9},{9,10},{10,11},{12,13},{... | collective-permute-start | bytes 7688 | tf_op jit(solution)/shard_map/ppermute | solution.py:18
  657.9 12.5 %collective-permute-start.42 = (f32[10,64,1]{2,1,0:T(8,128)S(1)}, f32[10,64,1]{2,1,0:T(8,128)S(1)}, u32[]{:S(2)}, u32[]{:S(2)}) collective-permute-start(f32[10,64,1]{2,1,0:T(8,128)S(1)} %get-tuple-element.306), channel_id=1, source_target_pairs={{1,0},{2,1},{3,2},{5,4},{6,5},{7,6},{9,8},{10,9},{11,10},{13,12},{... | collective-permute-start | bytes 7688 | tf_op jit(solution)/shard_map/ppermute | solution.py:19
  (110 other events, 752.2 us)
where the time goes:
time: 683 us; the launch traced here: 672 us
  blocking collectives  286 us (42%)
  waiting for transfers between devices  119 us (17%)
  starting transfers between devices  111 us (16%)
  other arithmetic  83.9 us (12%)
  local copies, waits for them, and re-layouts  42.6 us (6%)
  between operations  29.6 us (4%)
    psum x4, blocking collectives, local(): proj = lax.psum(local_dots, ('sx', 'sy'))  127 us
    psum x4, blocking collectives, local(): new_len = jnp.sqrt(lax.psum(jnp.sum(image * image), ('sx', 'sy')))  122 us
    ppermute x22, starting transfers between devices, extended(): before = lax.ppermute(last, axis, up)  81.9 us
    ppermute x22, waiting for transfers between devices, extended(): after = lax.ppermute(initial, axis, down)  72.8 us
    ppermute x22, waiting for transfers between devices, extended(): before = lax.ppermute(last, axis, up)  46 us
    psum x1, blocking collectives, local(): beta = jnp.sqrt(lax.psum(jnp.sum(rhs_field * rhs_field), ('sx', 'sy')))  36.6 us
    ppermute x22, starting transfers between devices, extended(): after = lax.ppermute(initial, axis, down)  28.9 us
    unnamed x232, local copies, waits for them, and re-layouts  21.9 us
  transfers between devices with their start and end apart: 44, of which 28 were waited for; matrix products, arithmetic and copies ran while one was open for 2% of the time, Pallas kernels for 0%

commit v1 on v0

v1 whole, which is shorter than its diff:
```python
import functools

import jax
import jax.numpy as jnp
from jax import lax
from jax.experimental import pallas as pl
from jax.experimental.pallas import tpu as pltpu
from jax.sharding import PartitionSpec as P

OV = 4
DEG = 3
M = 4
B = 8
MESH = pl.DeviceIdType.MESH
F32 = jnp.float32


def swap(a):
    return pltpu.roll(a, 64, a.ndim - 1)


def half_turn(a):
    return pltpu.roll(a, 4, a.ndim - 2)


def kernel(
    nsx, nsy, rhs_ref, cond_ref, inter_ref, coef_ref, sol_ref, res_ref,
    rc, kc, vb, qb, zb, sc, zc,
    fxp, fxm, fyp, fym, fzp, fzm, dg, inv, kx,
    ua, na, ub, nb, uc, nc, zx,
    pack, recx, recy, kxr, kyr, red1, red2,
    sem_sx, sem_rx, sem_sy, sem_ry, sem_ksx, sem_krx, sem_ksy, sem_kry,
    sem_s1, sem_r1, sem_s2, sem_r2,
):
    ix = lax.axis_index("sx")
    iy = lax.axis_index("sy")
    sub3 = lax.broadcasted_iota(jnp.int32, (1, 8, 128), 1)
    lane3 = lax.broadcasted_iota(jnp.int32, (1, 8, 128), 2)
    sub2 = lax.broadcasted_iota(jnp.int32, (8, 128), 0)
    own = lane3 < 64
    low = sub3 < 4
    depth = lane3 % 64

    def full(mask, size):
        return jnp.broadcast_to(mask, (size, 8, 128))

    recx[...] = jnp.zeros_like(recx)
    recy[...] = jnp.zeros_like(recy)
    kxr[...] = jnp.zeros_like(kxr)
    kyr[...] = jnp.zeros_like(kyr)

    def exists(dx, dy):
        return (ix + dx >= 0) & (ix + dx < nsx) & (iy + dy >= 0) & (iy + dy < nsy)

    def device(dx, dy):
        return {"sx": ix + dx, "sy": iy + dy}

    barrier = pltpu.get_barrier_semaphore()
    for d in range(1, nsx):
        pl.semaphore_signal(barrier, inc=1, device_id={"sx": lax.rem(ix + d, nsx), "sy": iy}, device_id_type=MESH)
    for d in range(1, nsy):
        pl.semaphore_signal(barrier, inc=1, device_id={"sx": ix, "sy": lax.rem(iy + d, nsy)}, device_id_type=MESH)
    corners = [(dx, dy) for dx in (-1, 1) for dy in (-1, 1)]
    for dx, dy in corners:
        @pl.when(exists(dx, dy))
        def _():
            pl.semaphore_signal(barrier, inc=1, device_id=device(dx, dy), device_id_type=MESH)

    def load_packed(src, dst):
        planes = []
        for x in range(8):
            a = src[x]
            both = jnp.concatenate([a[:, :64], a[:, 64:]], axis=0)
            planes.append(both.T)
        dst[...] = jnp.swapaxes(jnp.stack(planes, axis=0), 0, 1)

    load_packed(cond_ref, kc)
    load_packed(rhs_ref, rc)
    for ref in (ua, na, ub, nb, uc, nc, zx):
        ref[0:1] = jnp.zeros((1, 8, 128), F32)
        ref[137:138] = jnp.zeros((1, 8, 128), F32)

    peers = nsx - 1 + nsy - 1
    for dx, dy in corners:
        peers = peers + exists(dx, dy).astype(jnp.int32)
    pl.semaphore_wait(barrier, peers)

    def x_copies(make):
        return [(exists(side, 0), exists(-side, 0), make(side, slot)) for slot, side in enumerate((-1, 1))]

    def y_copies(make):
        out = []
        for slot, (dx, dy) in enumerate([(dx, dy) for dy in (-1, 1) for dx in (-1, 0, 1)]):
            out.append((exists(dx, dy), exists(-dx, -dy), make(dx, dy, slot)))
        return out

    def k_copies():
        def make_x(side, slot):
            return pltpu.make_async_remote_copy(
                kc, kxr.at[slot], sem_ksx.at[slot], sem_krx.at[slot],
                device_id=device(side, 0), device_id_type=MESH)

        def make_y(dx, dy, slot):
            src = kc.at[pl.ds(0, OV + 1)] if dy < 0 else kc.at[pl.ds(64 - OV - 1, OV + 1)]
            return pltpu.make_async_remote_copy(
                src, kyr.at[slot], sem_ksy.at[slot], sem_kry.at[slot],
                device_id=device(dx, dy), device_id_type=MESH)

        return x_copies(make_x) + y_copies(make_y)

    def f_copies(phase, field):
        def make_x(side, slot):
            return pltpu.make_async_remote_copy(
                pack.at[phase, slot], recx.at[phase, slot], sem_sx.at[phase, slot], sem_rx.at[phase, slot],
                device_id=device(side, 0), device_id_type=MESH)

        def make_y(dx, dy, slot):
            src = field.at[pl.ds(0, OV)] if dy < 0 else field.at[pl.ds(64 - OV, OV)]
            return pltpu.make_async_remote_copy(
                src, recy.at[phase, slot], sem_sy.at[phase, slot], sem_ry.at[phase, slot],
                device_id=device(dx, dy), device_id_type=MESH)

        return x_copies(make_x) + y_copies(make_y)

    def start(copies):
        for sends, _, copy in copies:
            pl.when(sends)(copy.start)

    def arrive(copies):
        for _, receives, copy in copies:
            pl.when(receives)(copy.wait_recv)

    def leave(copies):
        for sends, _, copy in copies:
            pl.when(sends)(copy.wait_send)

    def red_copies(phase, stage, sending):
        buf, ssem, rsem, n, me = (
            (red1, sem_s1, sem_r1, nsx, ix) if stage == 0 else (red2, sem_s2, sem_r2, nsy, iy))
        out = []
        for d in range(1, n):
            other = lax.rem(me + d, n)
            where = {"sx": other, "sy": iy} if stage == 0 else {"sx": ix, "sy": other}
            slot = me if sending else other
            out.append(pltpu.make_async_remote_copy(
                buf.at[phase, slot], buf.at[phase, slot], ssem.at[phase, d], rsem.at[phase, slot],
                device_id=where, device_id_type=MESH))
        return out

    def red_start(phase, stage, tile):
        if stage == 0:
            red1[phase, ix] = tile
        else:
            red2[phase, iy] = tile
        for copy in red_copies(phase, stage, True):
            copy.start()

    def red_finish(phase, stage):
        for copy in red_copies(phase, stage, False):
            copy.wait_recv()
        buf, n = (red1, nsx) if stage == 0 else (red2, nsy)
        total = buf[phase, 0]
        for i in range(1, n):
            total = total + buf[phase, i]
        return total

    def tile_of(accs):
        tile = jnp.zeros((8, 128), F32)
        for i, acc in enumerate(accs):
            tile = jnp.where(sub2 == i, jnp.broadcast_to(jnp.sum(acc, axis=0, keepdims=True), (8, 128)), tile)
        return tile

    def rows_of(total, n):
        sums = jnp.broadcast_to(jnp.sum(total, axis=1, keepdims=True), (8, 128))
        return [jnp.broadcast_to(sums[i:i + 1], (8, 128)) for i in range(n)]

    def pack_pair(phase, i, lo, hi):
        size = lo.shape[0]
        pack[phase, 0, pl.ds(i, size)] = jnp.where(full(low, size), lo, half_turn(hi))
        pack[phase, 1, pl.ds(i, size)] = jnp.where(full(low, size), half_turn(lo), hi)

    def loop(n, body, carry=None):
        return lax.fori_loop(0, n, body, carry)

    def ring_pair(c, r):
        size = c.shape[0]
        o = full(own, size)
        mixed = swap(jnp.where(o, r, c))
        return jnp.where(o, c, mixed), jnp.where(o, mixed, r)

    def ring_sides(buf, size):
        o, lo = full(own, size), full(low, size)
        above = jnp.where(o, buf[1], swap(jnp.where(lo, buf[0], buf[2])))
        below = jnp.where(o, swap(buf[4]), jnp.where(lo, buf[3], buf[5]))
        return above, below

    kcop = k_copies()
    start(kcop)

    def first(i, acc):
        lo = rc[pl.ds(i * B, B)]
        hi = rc[pl.ds(i * B + 32, B)]
        pack_pair(0, i * B, lo, hi)
        return acc + jnp.sum(lo * lo + hi * hi, axis=0)

    acc = loop(32 // B, first, jnp.zeros((8, 128), F32))
    copies = [f_copies(0, rc)]
    start(copies[0])
    red_start(0, 0, tile_of([acc]))

    arrive(kcop)

    def k_ring(i, _):
        c = kc[pl.ds(i * B, B)]
        r = jnp.where(full(low, B), kxr[0, pl.ds(i * B, B)], kxr[1, pl.ds(i * B, B)])
        a, b = ring_pair(c, r)
        kx[pl.ds(i * B + 5, B)] = a
        kx[pl.ds(i * B + 69, B)] = b
        return None

    loop(64 // B, k_ring)
    above, below = ring_sides(kyr, OV + 1)
    kx[133:138] = above
    kx[0:5] = below

    def far(i, slot):
        return kxr[slot, pl.ds(i, B)]

    def x_plus(a, size):
        return pltpu.roll(jnp.where(full(sub3 == 0, size), swap(a), a), 7, 1)

    def x_minus(a, size):
        return pltpu.roll(jnp.where(full(sub3 == 7, size), swap(a), a), 1, 1)

    end_plus = (lane3 >= 64) & (sub3 == 3)
    end_minus = (lane3 >= 64) & (sub3 == 4)
    top = depth == 63
    bottom = depth == 0

    def coefficients(at, size, beyond_plus, beyond_minus):
        k = kx[pl.ds(at, size)]
        kxp = jnp.where(full(end_plus, size), beyond_plus, x_plus(k, size))
        kxm = jnp.where(full(end_minus, size), beyond_minus, x_minus(k, size))
        kzp = jnp.where(full(top, size), 0.0, pltpu.roll(k, 127, 2))
        kzm = jnp.where(full(bottom, size), 0.0, pltpu.roll(k, 1, 2))
        xp = 0.5 * (k + kxp)
        xm = 0.5 * (k + kxm)
        yp = 0.5 * (k + kx[pl.ds(at + 1, size)])
        ym = 0.5 * (k + kx[pl.ds(at - 1, size)])
        zp = 0.5 * (k + kzp)
        zm = 0.5 * (k + kzm)
        diag = xp + xm + yp + ym + zp + zm
        inside = k > 0
        recip = jnp.where(inside, 1.0 / jnp.where(inside, diag, 1.0), 0.0)
        put = pl.ds(at, size)
        fxp[put] = xp * recip
        fxm[put] = xm * recip
        fyp[put] = yp * recip
        fym[put] = ym * recip
        fzp[put] = jnp.where(full(top, size), 0.0, zp * recip)
        fzm[put] = jnp.where(full(bottom, size), 0.0, zm * recip)
        inv[put] = recip
        dg[put] = jnp.where(full(own, size), diag, 0.0)

    def coef_body(i, _):
        p = pltpu.roll(kxr[0, pl.ds(i * B, B)], 7, 1)
        m = pltpu.roll(kxr[1, pl.ds(i * B, B)], 1, 1)
        coefficients(i * B + 5, B, swap(p), swap(m))
        coefficients(i * B + 69, B, p, m)
        return None

    loop(64 // B, coef_body)
    coefficients(133, 4, swap(pltpu.roll(kyr[0, 0:4], 7, 1)), swap(pltpu.roll(kyr[2, 0:4], 1, 1)))
    coefficients(1, 4, pltpu.roll(kyr[3, 1:5], 7, 1), pltpu.roll(kyr[5, 1:5], 1, 1))

    before = jnp.maximum(ix - 1, 0)
    after = jnp.minimum(ix + 1, nsx - 1)
    left, right = inter_ref[ix, 0], inter_ref[ix, 1]
    right_before, left_after = inter_ref[before, 1], inter_ref[after, 0]
    keep = own | (low & (sub3 < right)) | ((sub3 >= 4) & (sub3 >= 8 - left))
    keep_near = (lane3 >= 64) | (low & (sub3 < right_before)) | ((sub3 >= 4) & (sub3 >= 8 - left_after))
    keep = jnp.where(keep, 1.0, 0.0).astype(F32)
    keep_near = jnp.where(keep_near, 1.0, 0.0).astype(F32)

    def neighbours(at, size, srcs):
        put = pl.ds(at, size)
        cs = [f[put] for f in (fxp, fxm, fyp, fym, fzp, fzm)]
        outs = []
        for src in srcs:
            a = src[put]
            sw = swap(a)
            xp = pltpu.roll(jnp.where(full(sub3 == 0, size), sw, a), 7, 1)
            xm = pltpu.roll(jnp.where(full(sub3 == 7, size), sw, a), 1, 1)
            s = cs[0] * xp + cs[1] * xm
            s = s + (cs[2] * src[pl.ds(at + 1, size)] + cs[3] * src[pl.ds(at - 1, size)])
            s = s + (cs[4] * pltpu.roll(a, 127, 2) + cs[5] * pltpu.roll(a, 1, 2))
            outs.append(a - s)
        return outs

    def precondition_image(phase):
        def begin(at, field):
            put = pl.ds(at, field.shape[0])
            u = field * inv[put]
            ua[put] = u * keep
            na[put] = u * keep_near

        field = rc if phase == 0 else qb.at[phase - 1]

        def enter(i, _):
            a, b = recx[phase, 0, pl.ds(i * B, B)], recx[phase, 1, pl.ds(i * B, B)]
            r_lo = jnp.where(full(low, B), a, half_turn(b))
            r_hi = jnp.where(full(low, B), half_turn(a), b)
            for base, r in ((0, r_lo), (32, r_hi)):
                f, g = ring_pair(field[pl.ds(i * B + base, B)], r)
                begin(i * B + base + 5, f)
                begin(i * B + base + 69, g)
            return None

        loop(32 // B, enter)
        above, below = ring_sides(recy.at[phase], OV)
        begin(133, above)
        begin(1, below)

        for src, dst in (((ua, na), (ub, nb)), ((ub, nb), (uc, nc))):
            def power(i, _):
                at = i * B + 1
                u, n = neighbours(at, B, src)
                dst[0][pl.ds(at, B)] = u * keep
                dst[1][pl.ds(at, B)] = n * keep_near
                return None

            loop(136 // B, power)

        def last(i, _):
            at = i * B + 1
            put = pl.ds(at, B)
            u, n = neighbours(at, B, (uc, nc))
            o = full(own, B)
            u3 = jnp.where(o, u, n)
            u2 = jnp.where(o, uc[put], nc[put])
            u1 = jnp.where(o, ub[put], nb[put])
            u0 = jnp.where(o, ua[put], na[put])
            zx[put] = coef_ref[0] * u0 + coef_ref[1] * u1 + coef_ref[2] * u2 + coef_ref[3] * u3
            return None

        loop(136 // B, last)

        def image(i, _):
            at = i * B + 5
            o = full(own, B)
            lo = neighbours(at, B, (zx,))[0] * dg[pl.ds(at, B)]
            hi = neighbours(at + 64, B, (zx,))[0] * dg[pl.ds(at + 64, B)]
            sc[pl.ds(i * B, B)] = jnp.where(o, lo, swap(hi))
            zc[pl.ds(i * B, B)] = jnp.where(o, zx[pl.ds(at, B)], swap(zx[pl.ds(at + 64, B)]))
            return None

        loop(64 // B, image)

    hcols = []
    beta = None
    for k in range(M):
        arrive(copies[k])
        red_start(k, 1, red_finish(k, 0))
        precondition_image(k)
        rows = rows_of(red_finish(k, 1), k + 1)
        if k == 0:
            beta = jnp.sqrt(rows[0])
            scale = 1.0 / beta
            h = []
        else:
            h = rows[:k]
            square = rows[k]
            for x in h:
                square = square - x * x
            length = jnp.sqrt(square)
            scale = 1.0 / length
            hcols.append(h + [length])

        def update(i, accs, k=k, h=h, scale=scale):
            accs = list(accs)
            fields = []
            for base in (0, 32):
                put = pl.ds(i * B + base, B)
                v = rc[put] if k == 0 else qb[k - 1, put]
                q = sc[put]
                z = zc[put]
                basis = [vb[j, put] for j in range(k)]
                for j in range(k):
                    v = v - h[j] * basis[j]
                    q = q - h[j] * qb[j, put]
                    z = z - h[j] * zb[j, put]
                v, q, z = v * scale, q * scale, z * scale
                vb[k, put] = v
                qb[k, put] = q
                zb[k, put] = z
                for j, b in enumerate(basis + [v, q]):
                    accs[j] = accs[j] + jnp.sum(q * b, axis=0)
                fields.append(q)
            if k < M - 1:
                pack_pair(k + 1, i * B, fields[0], fields[1])
            return tuple(accs)

        accs = loop(32 // B, update, tuple(jnp.zeros((8, 128), F32) for _ in range(k + 2)))
        if k < M - 1:
            copies.append(f_copies(k + 1, qb.at[k]))
            start(copies[k + 1])
        red_start(k + 1, 0, tile_of(accs))

    red_start(M, 1, red_finish(M, 0))
    rows = rows_of(red_finish(M, 1), M + 1)
    square = rows[M]
    for x in rows[:M]:
        square = square - x * x
    hcols.append(rows[:M] + [jnp.sqrt(square)])

    g = [beta] + [jnp.zeros((8, 128), F32)] * M
    turns = []
    upper = []
    for k in range(M):
        col = list(hcols[k])
        for j, (c, s) in enumerate(turns):
            col[j], col[j + 1] = c * col[j] + s * col[j + 1], c * col[j + 1] - s * col[j]
        rad = jnp.sqrt(col[k] * col[k] + col[k + 1] * col[k + 1])
        c, s = col[k] / rad, col[k + 1] / rad
        turns.append((c, s))
        col[k] = c * col[k] + s * col[k + 1]
        upper.append(col)
        g[k], g[k + 1] = c * g[k] + s * g[k + 1], c * g[k + 1] - s * g[k]
    y = [None] * M
    for k in reversed(range(M)):
        run = g[k]
        for later in range(k + 1, M):
            run = run - upper[later][k] * y[later]
        y[k] = run / upper[k][k]

    def combine(i, _):
        put = pl.ds(i * B, B)
        z = y[0] * zb[0, put]
        r = rc[put] - y[0] * qb[0, put]
        for k in range(1, M):
            z = z + y[k] * zb[k, put]
            r = r - y[k] * qb[k, put]
        zc[put] = z
        sc[put] = r
        return None

    loop(64 // B, combine)

    def store_packed(src, dst):
        planes = jnp.swapaxes(src[...], 0, 1)
        for x in range(8):
            t = planes[x].T
            dst[x] = jnp.concatenate([t[:64], t[64:]], axis=1)

    store_packed(zc, sol_ref)
    store_packed(sc, res_ref)

    leave(kcop)
    for c in copies:
        leave(c)
    for phase in range(M + 1):
        for stage in range(2):
            for copy in red_copies(phase, stage, True):
                copy.wait_send()


def local(nsx, nsy, rhs_field, conduct, intersections, poly_coef):
    assert rhs_field.shape == (8, 64, 128)
    vmem = pl.BlockSpec(memory_space=pltpu.VMEM)
    smem = pl.BlockSpec(memory_space=pltpu.SMEM)
    packed = (64, 8, 128)
    ring = (138, 8, 128)
    dma = pltpu.SemaphoreType.DMA
    scratch = (
        [pltpu.VMEM(packed, F32)] * 2
        + [pltpu.VMEM((M,) + packed, F32)] * 3
        + [pltpu.VMEM(packed, F32)] * 2
        + [pltpu.VMEM(ring, F32)] * 16
        + [
            pltpu.VMEM((M, 2, 32, 8, 128), F32),
            pltpu.VMEM((M, 2, 32, 8, 128), F32),
            pltpu.VMEM((M, 6, OV, 8, 128), F32),
            pltpu.VMEM((2,) + packed, F32),
            pltpu.VMEM((6, OV + 1, 8, 128), F32),
            pltpu.VMEM((M + 1, nsx, 8, 128), F32),
            pltpu.VMEM((M + 1, nsy, 8, 128), F32),
            dma((M, 2)), dma((M, 2)), dma((M, 6)), dma((M, 6)),
            dma((2,)), dma((2,)), dma((6,)), dma((6,)),
            dma((M + 1, nsx)), dma((M + 1, nsx)), dma((M + 1, nsy)), dma((M + 1, nsy)),
        ]
    )
    out = jax.ShapeDtypeStruct(rhs_field.shape, F32)
    return pl.pallas_call(
        functools.partial(kernel, nsx, nsy),
        out_shape=(out, out),
        in_specs=[vmem, vmem, smem, smem],
        out_specs=(vmem, vmem),
        scratch_shapes=scratch,
        compiler_params=pltpu.CompilerParams(
            collective_id=0, has_side_effects=True, vmem_limit_bytes=40 * 1024 * 1024
        ),
        name="gmres_cycle",
    )(rhs_field, conduct, intersections, poly_coef)


def solution(mesh):
    nsx, nsy = mesh.shape["sx"], mesh.shape["sy"]
    spec = P(("grp", "sx"), None, "sy")
    return jax.shard_map(
        functools.partial(local, nsx, nsy),
        mesh=mesh,
        in_specs=(spec, spec, P("grp", None), P()),
        out_specs=(spec, spec),
        check_vma=False,
    )
```

time: 683 us -> 73.5 us (0.11); the launches traced: 672 us -> 73.3 us
  blocking collectives: 286 us -> 0 us
  waiting for transfers between devices: 119 us -> 0 us
  starting transfers between devices: 111 us -> 0 us
  other arithmetic: 83.9 us -> 0 us
  Pallas kernels: 0 us -> 68.6 us
  local copies, waits for them, and re-layouts: 42.6 us -> 4.08 us
  between operations: 29.6 us -> 0.65 us
    psum x9 -> x0, blocking collectives: 286 us -> none  [the longest x4 127 us: local(): proj = lax.psum(local_dots, ('sx', 'sy'))]
    ppermute x44 -> x0, waiting for transfers between devices: 119 us -> none  [the longest x22 72.8 us: extended(): after = lax.ppermute(initial, axis, down)]
    ppermute x44 -> x0, starting transfers between devices: 111 us -> none  [the longest x22 81.9 us: extended(): before = lax.ppermute(last, axis, up)]
    pallas_call x0 -> x1, Pallas kernels: none -> 68.6 us  [local(): pl.pallas_call(functools.partial(kernel, nsx, nsy), out_shape=(out, out),...]
    reduce_sum x9 -> x0, other arithmetic: 25.3 us -> none  [the longest x4 13.7 us: local(): new_len = jnp.sqrt(lax.psum(jnp.sum(image * image), ('sx', 'sy')))]
    select_n x15 -> x0, other arithmetic: 24.4 us -> none  [the longest x10 19.6 us: precondition(): jnp.where(mask_now, five_point_operator(padded, kdeep[:, :, power:power +...]
    slice x57 -> x0, local copies, waits for them, and re-layouts: 18.2 us -> none  [the longest x10 3.35 us: five_point_operator(): center_vector = padded_vector[1:-1, :, 1:-1]]
    add x14 -> x0, other arithmetic: 18.2 us -> none  [the longest x5 14.5 us: precondition(): result + poly_coef[power] * level[OV:OV + width_x, :, margin:margin + ver...]
  transfers between devices with their start and end apart: 44 -> 0, of which waited for: 28 -> 0; matrix products, arithmetic and copies ran while one was open for 2% -> 0% of each run, Pallas kernels for 0% -> 0%
where the time goes in v1:
time: 73.5 us; the launch traced here: 73.3 us
  Pallas kernels  68.6 us (93%)
  local copies, waits for them, and re-layouts  4.08 us (6%)
    pallas_call x1, Pallas kernels, local(): pl.pallas_call(functools.partial(kernel, nsx, nsy), out_shape=(out, out),...  68.6 us
    unnamed x9, local copies, waits for them, and re-layouts  4.08 us

profile of v1, /device:TPU:0, one launch (start us, length us, event | category | flops | bytes accessed | tf_op | source)
XLA Modules:
  0.0 73.3 jit_solution(8005811812892372173)
XLA Ops:
  0.6 0.0 copy-start.2
  0.6 0.8 %copy.6.inter_ref = s32[4,2]{1,0:T(4,128)S(1)} copy(s32[4,2]{0,1:T(2,128)} %param.6) | data formatting | bytes 64 | tf_op args[2]
  1.4 0.0 copy-done.2
  1.4 0.0 copy-start
  1.4 0.9 %copy-done = f32[8,64,128]{2,1,0:T(8,128)S(1)} copy-done((f32[8,64,128]{2,1,0:T(8,128)S(1)}, f32[8,64,128]{2,1,0:T(8,128)}, u32[]{:S(2)}) %copy-start) | copy-done | bytes 262168
  2.4 0.0 copy-start.1
  2.4 0.9 %copy-done.1 = f32[8,64,128]{2,1,0:T(8,128)S(1)} copy-done((f32[8,64,128]{2,1,0:T(8,128)S(1)}, f32[8,64,128]{2,1,0:T(8,128)}, u32[]{:S(2)}) %copy-start.1) | copy-done | bytes 262168
  3.3 68.6 %gmres_cycle.1 = (f32[8,64,128]{2,1,0:T(8,128)S(1)}, f32[8,64,128]{2,1,0:T(8,128)S(1)}) custom-call(f32[8,64,128]{2,1,0:T(8,128)S(1)} %copy-done, f32[8,64,128]{2,1,0:T(8,128)S(1)} %copy-done.1, s32[4,2]{1,0:T(4,128)S(1)} %copy.6.inter_ref, f32[4]{0:T(128)S(1)} %copy-done.2), custom_call_target="tpu_custom_call" | custom-call | tf_op jit(solution)/shard_map/gmres_cycle/pallas_call | solution.py:493
  71.9 0.7 copy.9
  72.6 0.7 copy.10
Async XLA Ops:
  0.6 0.8 %copy-start.2 = (f32[4]{0:T(128)S(1)}, f32[4]{0:T(128)}, u32[]{:S(2)}) copy-start(f32[4]{0:T(128)} %coef_ref.1) | copy-start | bytes 52
  1.4 1.0 %copy-start = (f32[8,64,128]{2,1,0:T(8,128)S(1)}, f32[8,64,128]{2,1,0:T(8,128)}, u32[]{:S(2)}) copy-start(f32[8,64,128]{2,1,0:T(8,128)} %rhs_ref.1) | copy-start | bytes 786436
  2.4 0.9 %copy-start.1 = (f32[8,64,128]{2,1,0:T(8,128)S(1)}, f32[8,64,128]{2,1,0:T(8,128)}, u32[]{:S(2)}) copy-start(f32[8,64,128]{2,1,0:T(8,128)} %cond_ref.1) | copy-start | bytes 786436

commit v2 on v1

--- a/solution.py
+++ b/solution.py
@@ -10,7 +10,8 @@
 OV = 4
 DEG = 3
 M = 4
-B = 8
+B = 32
+PB = 34
 MESH = pl.DeviceIdType.MESH
 F32 = jnp.float32
 
@@ -28,7 +29,7 @@
     rc, kc, vb, qb, zb, sc, zc,
     fxp, fxm, fyp, fym, fzp, fzm, dg, inv, kx,
     ua, na, ub, nb, uc, nc, zx,
-    pack, recx, recy, kxr, kyr, red1, red2,
+    pack, ypack, recx, recy, kxr, kyr, red1, red2,
     sem_sx, sem_rx, sem_sy, sem_ry, sem_ksx, sem_krx, sem_ksy, sem_kry,
     sem_s1, sem_r1, sem_s2, sem_r2,
 ):
@@ -37,12 +38,25 @@
     sub3 = lax.broadcasted_iota(jnp.int32, (1, 8, 128), 1)
     lane3 = lax.broadcasted_iota(jnp.int32, (1, 8, 128), 2)
     sub2 = lax.broadcasted_iota(jnp.int32, (8, 128), 0)
-    own = lane3 < 64
-    low = sub3 < 4
-    depth = lane3 % 64
+
+    def own(s, l):
+        return l < 64
+
+    def low(s, l):
+        return s < 4
+
+    def middle(s, l):
+        return (s == 3) | (s == 4)
+
+    def first_sub(s, l):
+        return s == 0
+
+    def last_sub(s, l):
+        return s == 7
 
     def full(mask, size):
-        return jnp.broadcast_to(mask, (size, 8, 128))
+        shape = (size, 8, 128)
+        return mask(lax.broadcasted_iota(jnp.int32, shape, 1), lax.broadcasted_iota(jnp.int32, shape, 2))
 
     recx[...] = jnp.zeros_like(recx)
     recy[...] = jnp.zeros_like(recy)
@@ -55,12 +69,22 @@
     def device(dx, dy):
         return {"sx": ix + dx, "sy": iy + dy}
 
+    direct = nsx * nsy <= 16
+    slots = nsx * nsy if direct else nsx
+    others = [(dx, dy) for dx in range(nsx) for dy in range(nsy) if (dx, dy) != (0, 0)]
+
+    def around(dx, dy):
+        return {"sx": lax.rem(ix + dx, nsx), "sy": lax.rem(iy + dy, nsy)}
+
     barrier = pltpu.get_barrier_semaphore()
-    for d in range(1, nsx):
+    if direct:
+        for dx, dy in others:
+            pl.semaphore_signal(barrier, inc=1, device_id=around(dx, dy), device_id_type=MESH)
+    for d in range(1, nsx if not direct else 0):
         pl.semaphore_signal(barrier, inc=1, device_id={"sx": lax.rem(ix + d, nsx), "sy": iy}, device_id_type=MESH)
-    for d in range(1, nsy):
+    for d in range(1, nsy if not direct else 0):
         pl.semaphore_signal(barrier, inc=1, device_id={"sx": ix, "sy": lax.rem(iy + d, nsy)}, device_id_type=MESH)
-    corners = [(dx, dy) for dx in (-1, 1) for dy in (-1, 1)]
+    corners = [] if direct else [(dx, dy) for dx in (-1, 1) for dy in (-1, 1)]
     for dx, dy in corners:
         @pl.when(exists(dx, dy))
         def _():
@@ -80,7 +104,7 @@
         ref[0:1] = jnp.zeros((1, 8, 128), F32)
         ref[137:138] = jnp.zeros((1, 8, 128), F32)
 
-    peers = nsx - 1 + nsy - 1
+    peers = len(others) if direct else nsx - 1 + nsy - 1
     for dx, dy in corners:
         peers = peers + exists(dx, dy).astype(jnp.int32)
     pl.semaphore_wait(barrier, peers)
@@ -108,16 +132,18 @@
 
         return x_copies(make_x) + y_copies(make_y)
 
-    def f_copies(phase, field):
+    def f_copies(phase):
         def make_x(side, slot):
             return pltpu.make_async_remote_copy(
                 pack.at[phase, slot], recx.at[phase, slot], sem_sx.at[phase, slot], sem_rx.at[phase, slot],
                 device_id=device(side, 0), device_id_type=MESH)
 
         def make_y(dx, dy, slot):
-            src = field.at[pl.ds(0, OV)] if dy < 0 else field.at[pl.ds(64 - OV, OV)]
+            strip = ypack.at[phase, 0 if dy < 0 else 1]
+            src = {0: strip.at[pl.ds(0, 2)], -1: strip.at[pl.ds(2, 1)], 1: strip.at[pl.ds(3, 1)]}[dx]
+            dst = recy.at[phase, slot] if dx == 0 else recy.at[phase, slot, pl.ds(0, 1)]
             return pltpu.make_async_remote_copy(
-                src, recy.at[phase, slot], sem_sy.at[phase, slot], sem_ry.at[phase, slot],
+                src, dst, sem_sy.at[phase, slot], sem_ry.at[phase, slot],
                 device_id=device(dx, dy), device_id_type=MESH)
 
         return x_copies(make_x) + y_copies(make_y)
@@ -135,6 +161,15 @@
             pl.when(sends)(copy.wait_send)
 
     def red_copies(phase, stage, sending):
+        if direct:
+            out = []
+            for dx, dy in others:
+                where = around(dx, dy)
+                slot = ix * nsy + iy if sending else where["sx"] * nsy + where["sy"]
+                out.append(pltpu.make_async_remote_copy(
+                    red1.at[phase, slot], red1.at[phase, slot], sem_s1.at[phase, dx * nsy + dy], sem_r1.at[phase, slot],
+                    device_id=where, device_id_type=MESH))
+            return out
         buf, ssem, rsem, n, me = (
             (red1, sem_s1, sem_r1, nsx, ix) if stage == 0 else (red2, sem_s2, sem_r2, nsy, iy))
         out = []
@@ -149,7 +184,7 @@
 
     def red_start(phase, stage, tile):
         if stage == 0:
-            red1[phase, ix] = tile
+            red1[phase, ix * nsy + iy if direct else ix] = tile
         else:
             red2[phase, iy] = tile
         for copy in red_copies(phase, stage, True):
@@ -158,11 +193,18 @@
     def red_finish(phase, stage):
         for copy in red_copies(phase, stage, False):
             copy.wait_recv()
-        buf, n = (red1, nsx) if stage == 0 else (red2, nsy)
-        total = buf[phase, 0]
-        for i in range(1, n):
-            total = total + buf[phase, i]
-        return total
+        buf, n = (red1, slots) if stage == 0 else (red2, nsy)
+        terms = [buf[phase, i] for i in range(n)]
+        while len(terms) > 1:
+            terms = [sum(terms[i:i + 2][1:], terms[i]) for i in range(0, len(terms), 2)]
+        return terms[0]
+
+    def red_middle(phase):
+        if not direct:
+            red_start(phase, 1, red_finish(phase, 0))
+
+    def red_end(phase):
+        return red_finish(phase, 0 if direct else 1)
 
     def tile_of(accs):
         tile = jnp.zeros((8, 128), F32)
@@ -179,6 +221,15 @@
         pack[phase, 0, pl.ds(i, size)] = jnp.where(full(low, size), lo, half_turn(hi))
         pack[phase, 1, pl.ds(i, size)] = jnp.where(full(low, size), half_turn(lo), hi)
 
+    def pack_strips(phase, field):
+        o = full(own, 2)
+        c, d = field[0:4], field[60:64]
+        for side, p in enumerate((jnp.where(o, c[0:2], swap(c[2:4])), jnp.where(o, swap(d[0:2]), d[2:4]))):
+            ypack[phase, side, 0:2] = p
+            lo = full(low, 1)
+            ypack[phase, side, 2:3] = jnp.where(lo, p[0:1], half_turn(p[1:2]))
+            ypack[phase, side, 3:4] = jnp.where(lo, half_turn(p[0:1]), p[1:2])
+
     def loop(n, body, carry=None):
         return lax.fori_loop(0, n, body, carry)
 
@@ -204,7 +255,8 @@
         return acc + jnp.sum(lo * lo + hi * hi, axis=0)
 
     acc = loop(32 // B, first, jnp.zeros((8, 128), F32))
-    copies = [f_copies(0, rc)]
+    pack_strips(0, rc)
+    copies = [f_copies(0)]
     start(copies[0])
     red_start(0, 0, tile_of([acc]))
 
@@ -227,15 +279,22 @@
         return kxr[slot, pl.ds(i, B)]
 
     def x_plus(a, size):
-        return pltpu.roll(jnp.where(full(sub3 == 0, size), swap(a), a), 7, 1)
+        return pltpu.roll(jnp.where(full(first_sub, size), swap(a), a), 7, 1)
 
     def x_minus(a, size):
-        return pltpu.roll(jnp.where(full(sub3 == 7, size), swap(a), a), 1, 1)
-
-    end_plus = (lane3 >= 64) & (sub3 == 3)
-    end_minus = (lane3 >= 64) & (sub3 == 4)
-    top = depth == 63
-    bottom = depth == 0
+        return pltpu.roll(jnp.where(full(last_sub, size), swap(a), a), 1, 1)
+
+    def end_plus(s, l):
+        return (l >= 64) & (s == 3)
+
+    def end_minus(s, l):
+        return (l >= 64) & (s == 4)
+
+    def top(s, l):
+        return l % 64 == 63
+
+    def bottom(s, l):
+        return l % 64 == 0
 
     def coefficients(at, size, beyond_plus, beyond_minus):
         k = kx[pl.ds(at, size)]
@@ -277,8 +336,8 @@
     after = jnp.minimum(ix + 1, nsx - 1)
     left, right = inter_ref[ix, 0], inter_ref[ix, 1]
     right_before, left_after = inter_ref[before, 1], inter_ref[after, 0]
-    keep = own | (low & (sub3 < right)) | ((sub3 >= 4) & (sub3 >= 8 - left))
-    keep_near = (lane3 >= 64) | (low & (sub3 < right_before)) | ((sub3 >= 4) & (sub3 >= 8 - left_after))
+    keep = (lane3 < 64) | ((sub3 < 4) & (sub3 < right)) | ((sub3 >= 4) & (sub3 >= 8 - left))
+    keep_near = (lane3 >= 64) | ((sub3 < 4) & (sub3 < right_before)) | ((sub3 >= 4) & (sub3 >= 8 - left_after))
     keep = jnp.where(keep, 1.0, 0.0).astype(F32)
     keep_near = jnp.where(keep_near, 1.0, 0.0).astype(F32)
 
@@ -286,13 +345,17 @@
         put = pl.ds(at, size)
         cs = [f[put] for f in (fxp, fxm, fyp, fym, fzp, fzm)]
         outs = []
+        if len(srcs) == 2:
+            both = swap(jnp.where(full(middle, size), half_turn(srcs[1][put]), srcs[0][put]))
+            sws = (both, half_turn(both))
         for src in srcs:
-            a = src[put]
-            sw = swap(a)
-            xp = pltpu.roll(jnp.where(full(sub3 == 0, size), sw, a), 7, 1)
-            xm = pltpu.roll(jnp.where(full(sub3 == 7, size), sw, a), 1, 1)
+            w = src[pl.ds(at - 1, size + 2)]
+            a = w[1:size + 1]
+            sw = swap(a) if len(srcs) == 1 else sws[src is srcs[1]]
+            xp = pltpu.roll(jnp.where(full(first_sub, size), sw, a), 7, 1)
+            xm = pltpu.roll(jnp.where(full(last_sub, size), sw, a), 1, 1)
             s = cs[0] * xp + cs[1] * xm
-            s = s + (cs[2] * src[pl.ds(at + 1, size)] + cs[3] * src[pl.ds(at - 1, size)])
+            s = s + (cs[2] * w[2:] + cs[3] * w[:size])
             s = s + (cs[4] * pltpu.roll(a, 127, 2) + cs[5] * pltpu.roll(a, 1, 2))
             outs.append(a - s)
         return outs
@@ -317,25 +380,30 @@
             return None
 
         loop(32 // B, enter)
-        above, below = ring_sides(recy.at[phase], OV)
-        begin(133, above)
-        begin(1, below)
+        lo = full(low, 1)
+        for slot, at in ((0, 133), (3, 1)):
+            p = recy[phase, slot + 1]
+            a, b = recy[phase, slot, 0:1], recy[phase, slot + 2, 0:1]
+            r = jnp.concatenate([jnp.where(lo, a, half_turn(b)), jnp.where(lo, half_turn(a), b)], axis=0)
+            f, g = ring_pair(p, r)
+            begin(at, f)
+            begin(at + 2, g)
 
         for src, dst in (((ua, na), (ub, nb)), ((ub, nb), (uc, nc))):
             def power(i, _):
-                at = i * B + 1
-                u, n = neighbours(at, B, src)
-                dst[0][pl.ds(at, B)] = u * keep
-                dst[1][pl.ds(at, B)] = n * keep_near
+                at = i * PB + 1
+                u, n = neighbours(at, PB, src)
+                dst[0][pl.ds(at, PB)] = u * keep
+                dst[1][pl.ds(at, PB)] = n * keep_near
                 return None
 
-            loop(136 // B, power)
+            loop(136 // PB, power)
 
         def last(i, _):
-            at = i * B + 1
-            put = pl.ds(at, B)
-            u, n = neighbours(at, B, (uc, nc))
-            o = full(own, B)
+            at = i * PB + 1
+            put = pl.ds(at, PB)
+            u, n = neighbours(at, PB, (uc, nc))
+            o = full(own, PB)
             u3 = jnp.where(o, u, n)
             u2 = jnp.where(o, uc[put], nc[put])
             u1 = jnp.where(o, ub[put], nb[put])
@@ -343,7 +411,7 @@
             zx[put] = coef_ref[0] * u0 + coef_ref[1] * u1 + coef_ref[2] * u2 + coef_ref[3] * u3
             return None
 
-        loop(136 // B, last)
+        loop(136 // PB, last)
 
         def image(i, _):
             at = i * B + 5
@@ -360,9 +428,9 @@
     beta = None
     for k in range(M):
         arrive(copies[k])
-        red_start(k, 1, red_finish(k, 0))
+        red_middle(k)
         precondition_image(k)
-        rows = rows_of(red_finish(k, 1), k + 1)
+        rows = rows_of(red_end(k), k + 1)
         if k == 0:
             beta = jnp.sqrt(rows[0])
             scale = 1.0 / beta
@@ -376,38 +444,57 @@
             scale = 1.0 / length
             hcols.append(h + [length])
 
-        def update(i, accs, k=k, h=h, scale=scale):
-            accs = list(accs)
+        def update_q(i, _, k=k, h=h, scale=scale):
             fields = []
             for base in (0, 32):
                 put = pl.ds(i * B + base, B)
+                q = sc[put]
+                for j in range(k):
+                    q = q - h[j] * qb[j, put]
+                q = q * scale
+                qb[k, put] = q
+                fields.append(q)
+            if k < M - 1:
+                pack_pair(k + 1, i * B, fields[0], fields[1])
+            return None
+
+        loop(32 // B, update_q)
+        if k < M - 1:
+            pack_strips(k + 1, qb.at[k])
+            copies.append(f_copies(k + 1))
+            start(copies[k + 1])
+
+        def update_v(i, accs, k=k, h=h, scale=scale):
+            accs = list(accs)
+            for base in (0, 32):
+                put = pl.ds(i * B + base, B)
                 v = rc[put] if k == 0 else qb[k - 1, put]
-                q = sc[put]
-                z = zc[put]
+                q = qb[k, put]
                 basis = [vb[j, put] for j in range(k)]
                 for j in range(k):
                     v = v - h[j] * basis[j]
-                    q = q - h[j] * qb[j, put]
-                    z = z - h[j] * zb[j, put]
-                v, q, z = v * scale, q * scale, z * scale
+                v = v * scale
                 vb[k, put] = v
-                qb[k, put] = q
-                zb[k, put] = z
                 for j, b in enumerate(basis + [v, q]):
                     accs[j] = accs[j] + jnp.sum(q * b, axis=0)
-                fields.append(q)
-            if k < M - 1:
-                pack_pair(k + 1, i * B, fields[0], fields[1])
             return tuple(accs)
 
-        accs = loop(32 // B, update, tuple(jnp.zeros((8, 128), F32) for _ in range(k + 2)))
-        if k < M - 1:
-            copies.append(f_copies(k + 1, qb.at[k]))
-            start(copies[k + 1])
+        accs = loop(32 // B, update_v, tuple(jnp.zeros((8, 128), F32) for _ in range(k + 2)))
         red_start(k + 1, 0, tile_of(accs))
 
-    red_start(M, 1, red_finish(M, 0))
-    rows = rows_of(red_finish(M, 1), M + 1)
+        def update_z(i, _, k=k, h=h, scale=scale):
+            for base in (0, 32):
+                put = pl.ds(i * B + base, B)
+                z = zc[put]
+                for j in range(k):
+                    z = z - h[j] * zb[j, put]
+                zb[k, put] = z * scale
+            return None
+
+        loop(32 // B, update_z)
+
+    red_middle(M)
+    rows = rows_of(red_end(M), M + 1)
     square = rows[M]
     for x in rows[:M]:
         square = square - x * x
@@ -459,7 +546,7 @@
     for c in copies:
         leave(c)
     for phase in range(M + 1):
-        for stage in range(2):
+        for stage in range(1 if direct else 2):
             for copy in red_copies(phase, stage, True):
                 copy.wait_send()
 
@@ -471,6 +558,7 @@
     packed = (64, 8, 128)
     ring = (138, 8, 128)
     dma = pltpu.SemaphoreType.DMA
+    slots = nsx * nsy if nsx * nsy <= 16 else nsx
     scratch = (
         [pltpu.VMEM(packed, F32)] * 2
         + [pltpu.VMEM((M,) + packed, F32)] * 3
@@ -478,15 +566,16 @@
         + [pltpu.VMEM(ring, F32)] * 16
         + [
             pltpu.VMEM((M, 2, 32, 8, 128), F32),
+            pltpu.VMEM((M, 2, OV, 8, 128), F32),
             pltpu.VMEM((M, 2, 32, 8, 128), F32),
-            pltpu.VMEM((M, 6, OV, 8, 128), F32),
+            pltpu.VMEM((M, 6, 2, 8, 128), F32),
             pltpu.VMEM((2,) + packed, F32),
             pltpu.VMEM((6, OV + 1, 8, 128), F32),
-            pltpu.VMEM((M + 1, nsx, 8, 128), F32),
+            pltpu.VMEM((M + 1, slots, 8, 128), F32),
             pltpu.VMEM((M + 1, nsy, 8, 128), F32),
             dma((M, 2)), dma((M, 2)), dma((M, 6)), dma((M, 6)),
             dma((2,)), dma((2,)), dma((6,)), dma((6,)),
-            dma((M + 1, nsx)), dma((M + 1, nsx)), dma((M + 1, nsy)), dma((M + 1, nsy)),
+            dma((M + 1, slots)), dma((M + 1, slots)), dma((M + 1, nsy)), dma((M + 1, nsy)),
         ]
     )
     out = jax.ShapeDtypeStruct(rhs_field.shape, F32)

time: 73.5 us -> 58.9 us (0.80)
  Pallas kernels: 68.6 us -> 53.9 us
    pallas_call x1, Pallas kernels: 68.6 us -> 53.9 us  [local(): pl.pallas_call(functools.partial(kernel, nsx, nsy), out_shape=(out, out),...]
where the time goes in v2:
time: 58.9 us; the launch traced here: 58.7 us
  Pallas kernels  53.9 us (92%)
  local copies, waits for them, and re-layouts  4.08 us (7%)
  between operations  0.65 us (1%)
    pallas_call x1, Pallas kernels, local(): pl.pallas_call(functools.partial(kernel, nsx, nsy), out_shape=(out, out),...  53.9 us
    unnamed x9, local copies, waits for them, and re-layouts  4.08 us

profile of v2, /device:TPU:0, one launch (start us, length us, event | category | flops | bytes accessed | tf_op | source)
XLA Modules:
  0.0 58.7 jit_solution(12091737471433581453)
XLA Ops:
  0.6 0.0 copy-start.2
  0.6 0.8 %copy.6.inter_ref = s32[4,2]{1,0:T(4,128)S(1)} copy(s32[4,2]{0,1:T(2,128)} %param.6) | data formatting | bytes 64 | tf_op args[2]
  1.4 0.0 copy-done.2
  1.4 0.0 copy-start
  1.4 0.9 %copy-done = f32[8,64,128]{2,1,0:T(8,128)S(1)} copy-done((f32[8,64,128]{2,1,0:T(8,128)S(1)}, f32[8,64,128]{2,1,0:T(8,128)}, u32[]{:S(2)}) %copy-start) | copy-done | bytes 262168
  2.4 0.0 copy-start.1
  2.4 0.9 %copy-done.1 = f32[8,64,128]{2,1,0:T(8,128)S(1)} copy-done((f32[8,64,128]{2,1,0:T(8,128)S(1)}, f32[8,64,128]{2,1,0:T(8,128)}, u32[]{:S(2)}) %copy-start.1) | copy-done | bytes 262168
  3.3 53.9 %gmres_cycle.1 = (f32[8,64,128]{2,1,0:T(8,128)S(1)}, f32[8,64,128]{2,1,0:T(8,128)S(1)}) custom-call(f32[8,64,128]{2,1,0:T(8,128)S(1)} %copy-done, f32[8,64,128]{2,1,0:T(8,128)S(1)} %copy-done.1, s32[4,2]{1,0:T(4,128)S(1)} %copy.6.inter_ref, f32[4]{0:T(128)S(1)} %copy-done.2), custom_call_target="tpu_custom_call" | custom-call | tf_op jit(solution)/shard_map/gmres_cycle/pallas_call | solution.py:582
  57.3 0.7 %copy.9 = f32[8,64,128]{2,1,0:T(8,128)} copy(f32[8,64,128]{2,1,0:T(8,128)S(1)} %get-tuple-element.4) | data formatting | bytes 524288
  58.0 0.7 %copy.10 = f32[8,64,128]{2,1,0:T(8,128)} copy(f32[8,64,128]{2,1,0:T(8,128)S(1)} %get-tuple-element.5) | data formatting | bytes 524288
Async XLA Ops:
  0.6 0.8 %copy-start.2 = (f32[4]{0:T(128)S(1)}, f32[4]{0:T(128)}, u32[]{:S(2)}) copy-start(f32[4]{0:T(128)} %coef_ref.1) | copy-start | bytes 52
  1.4 1.0 %copy-start = (f32[8,64,128]{2,1,0:T(8,128)S(1)}, f32[8,64,128]{2,1,0:T(8,128)}, u32[]{:S(2)}) copy-start(f32[8,64,128]{2,1,0:T(8,128)} %rhs_ref.1) | copy-start | bytes 786436
  2.4 0.9 %copy-start.1 = (f32[8,64,128]{2,1,0:T(8,128)S(1)}, f32[8,64,128]{2,1,0:T(8,128)}, u32[]{:S(2)}) copy-start(f32[8,64,128]{2,1,0:T(8,128)} %cond_ref.1) | copy-start | bytes 786436
